TPU v7x, 32 devices: a whole 2x2x4 slice. The times are simulated.
32 devices in a mesh: dp: 8 (over z, x), mp: 4 (over y, core).
Axes of the slice: x: 2, y: 2, z: 4, core: 2. Of those that a mesh axis runs over, the one named last changes fastest.
Arguments:
- token_ids: int32 [64, 128], P(('dp', 'mp')), may hold values from 0 to 31999, as said below
- levels: int32 [64], P(('dp', 'mp')), may hold values from 0 to 63
- noise: bfloat16 [64, 128, 256], P(('dp', 'mp')), may hold values from -6 to 6
- cotangent: bfloat16 [64, 128, 1024], P(('dp', 'mp'))
- table: float32 [32000, 256], P('dp'), may hold values from -6 to 6
- table_m: float32 [32000, 256], P('dp'), may hold values from -0.625 to 0.625
- table_v: float32 [32000, 256], P('dp'), may hold values from 0.0001024 to 0.001536
- w_in: float32 [256, 1024], P('dp'), may hold values from -0.375 to 0.375
- w_in_m: float32 [256, 1024], P('dp'), may hold values from -80 to 80
- w_in_v: float32 [256, 1024], P('dp'), may hold values from 7.3728 to 114.688
- ln_params: float32 [4, 1024], P(None, 'dp'), as said below
- ln_m: float32 [4, 1024], P(None, 'dp'), may hold values from -64 to 64
- ln_v: float32 [4, 1024], P(None, 'dp'), may hold values from 4.096 to 65.536
- w_qkv: float32 [3, 1024, 1024], P(None, 'dp', 'mp'), may hold values from -0.1875 to 0.1875
- qkv_m: float32 [3, 1024, 1024], P(None, 'dp', 'mp'), may hold values from -64 to 64
- qkv_v: float32 [3, 1024, 1024], P(None, 'dp', 'mp'), may hold values from 4.096 to 65.536
- w_out: float32 [1024, 1024], P('mp', 'dp'), may hold values from -0.75 to 0.75
- out_m: float32 [1024, 1024], P('mp', 'dp'), may hold values from -16 to 16
- out_v: float32 [1024, 1024], P('mp', 'dp'), may hold values from 0.4096 to 5.7344
- w_up: float32 [1024, 4096], P('dp', 'mp'), may hold values from -0.1875 to 0.1875
- up_m: float32 [1024, 4096], P('dp', 'mp'), may hold values from -16 to 16
- up_v: float32 [1024, 4096], P('dp', 'mp'), may hold values from 0.24576 to 4.096
- w_down: float32 [4096, 1024], P('mp', 'dp'), may hold values from -0.09375 to 0.09375
- down_m: float32 [4096, 1024], P('mp', 'dp'), may hold values from -32 to 32
- down_v: float32 [4096, 1024], P('mp', 'dp'), may hold values from 0.98304 to 16.384
Outputs:
- output: float32 [64, 128, 1024], P(('dp', 'mp'))
- table_new: float32 [32000, 256], P('dp')
- table_m_new: float32 [32000, 256], P('dp')
- table_v_new: float32 [32000, 256], P('dp')
- w_in_new: float32 [256, 1024], P('dp')
- w_in_m_new: float32 [256, 1024], P('dp')
- w_in_v_new: float32 [256, 1024], P('dp')
- ln_new: float32 [4, 1024], P(None, 'dp')
- ln_m_new: float32 [4, 1024], P(None, 'dp')
- ln_v_new: float32 [4, 1024], P(None, 'dp')
- qkv_new: float32 [3, 1024, 1024], P(None, 'dp', 'mp')
- qkv_m_new: float32 [3, 1024, 1024], P(None, 'dp', 'mp')
- qkv_v_new: float32 [3, 1024, 1024], P(None, 'dp', 'mp')
- out_new: float32 [1024, 1024], P('mp', 'dp')
- out_m_new: float32 [1024, 1024], P('mp', 'dp')
- out_v_new: float32 [1024, 1024], P('mp', 'dp')
- up_new: float32 [1024, 4096], P('dp', 'mp')
- up_m_new: float32 [1024, 4096], P('dp', 'mp')
- up_v_new: float32 [1024, 4096], P('dp', 'mp')
- down_new: float32 [4096, 1024], P('mp', 'dp')
- down_m_new: float32 [4096, 1024], P('mp', 'dp')
- down_v_new: float32 [4096, 1024], P('mp', 'dp')
- norms: float32 [2, 12], replicated
Inputs may be any that keep to these rules, and one draw needn't show every extreme that they name: `token_ids`: of the 256 tokens of one device, at most 48 name rows among the 4000 rows held by one index of dp, and in every draw some index of dp is named by exactly 48 tokens of every device. `ln_params`: rows 0 and 2 are positive gains.
All inputs are finite; a program needn't handle non-finite values.
Results may differ from a plain program's by a relative error of at most 0.025.
Values may be sent and summed in bfloat16 or wider, within the bound.
A program may use at most 192 MiB of HBM per device.

v0:
```python
import functools
import types

import jax
import jax.numpy as jnp
from jax import lax
from jax.experimental import pallas as pl
from jax.experimental.pallas import tpu as pltpu
from jax.sharding import PartitionSpec as P

HD = 64
LEVELS = 64
STEP = 10


EPS_NORM = 1e-06
EPS_LAYER = 1e-05
EPS_ADAM = 1e-06
BETA_ONE = 0.9
BETA_TWO = 0.999
DECAY = 0.01
RATE = 0.5
SIGMA_TOP = 10.0

F32 = jnp.float32
LOW = jnp.bfloat16
VMEM_BYTES = 63 * 1024 * 1024


def sigma_of(levels):
    frac = levels.astype(jnp.float32) / (LEVELS - 1)
    return jnp.exp(frac * jnp.log(SIGMA_TOP))


def lamb_moments(weight, gradient, first, second):
    first_new = BETA_ONE * first + (1.0 - BETA_ONE) * gradient
    second_new = BETA_TWO * second + (1.0 - BETA_TWO) * gradient * gradient
    first_hat = first_new / (1.0 - BETA_ONE**STEP)
    second_hat = second_new / (1.0 - BETA_TWO**STEP)
    direction = first_hat / (jnp.sqrt(second_hat) + EPS_ADAM) + DECAY * weight
    return (first_new, second_new, direction)


def trust_factors(ratio):
    return (
        ratio[0],
        ratio[1],
        ratio[2:6][:, None],
        ratio[6:9][:, None, None],
        ratio[9],
        ratio[10],
        ratio[11],
    )


def round_up(value, step):
    return -(-value // step) * step


def dot(left, right):
    return jnp.dot(left, right, preferred_element_type=F32)


def dot_nt(left, right):
    return lax.dot_general(left, right, (((1,), (1,)), ((), ())), preferred_element_type=F32)


def dot_tn(left, right):
    return lax.dot_general(left, right, (((0,), (0,)), ((), ())), preferred_element_type=F32)


def strips(total, step, body, unroll=1):
    step = min(step, total)

    def one(turn, carry):
        body(pl.multiple_of(turn * step, step))
        return carry

    lax.fori_loop(0, total // step, one, 0, unroll=unroll)


class Line:
    def __init__(self, axis):
        self.axis = axis
        self.size = lax.axis_size(axis)
        self.far = self.size // 2
        self.me = lax.axis_index(axis)
        self.hi = lax.div(self.me, 2)
        self.lo = lax.rem(self.me, 2)
        self.partner = self.hi * 2 + (1 - self.lo)

    def at(self, step):
        return lax.rem(self.hi + step + self.far, self.far)

    def push(self, index, src, dst, send, recv):
        return pltpu.make_async_remote_copy(
            src_ref=src,
            dst_ref=dst,
            send_sem=send,
            recv_sem=recv,
            device_id={self.axis: index},
            device_id_type=pl.DeviceIdType.MESH,
        )

    def signal(self, sem, index):
        pl.semaphore_signal(
            sem, inc=1, device_id={self.axis: index}, device_id_type=pl.DeviceIdType.MESH
        )


def meet(pair_lines, all_lines=()):
    sem = pltpu.get_barrier_semaphore()
    count = 0
    for line in pair_lines:
        for step in range(1, line.far):
            line.signal(sem, line.at(step) * 2 + line.lo)
            count += 1
        line.signal(sem, line.partner)
        count += 1
    for line in all_lines:
        for step in range(1, line.size):
            line.signal(sem, lax.rem(line.me + step, line.size))
            count += 1
    pl.semaphore_wait(sem, count)


class Gather:
    def __init__(self, line, at, send, recv, base=0, ends=False):
        self.line, self.at, self.send, self.recv, self.base = line, at, send, recv, base
        self.ends = ends and line.far == 4

    def source(self, step):
        line = self.line
        if not self.ends:
            return line.at(-step)
        order = ((1, 2, 3), (0, 3, 2), (3, 0, 1), (2, 1, 0))
        hi = order[3][step - 1]
        for place in (2, 1, 0):
            hi = jnp.where(line.hi == place, order[place][step - 1], hi)
        return hi

    def far_sends(self, act):
        line = self.line
        for step in range(1, line.far):
            one = self.copy(line.me, step - 1, line.at(step) * 2 + line.lo)
            if self.ends and step != 2:
                pl.when(line.hi != (3 if step == 1 else 0))(functools.partial(act, one))
            else:
                act(one)

    def to_end(self, act):
        line = self.line
        dest = jnp.where(line.hi == 1, 0, 3)
        one = self.copy((3 - dest) * 2 + line.lo, 2 * line.far - 1, dest * 2 + line.lo)
        pl.when((line.hi == 1) | (line.hi == 2))(functools.partial(act, one))

    def copy(self, index, slot, dest):
        block = self.at(index)
        return self.line.push(
            dest, block, block, self.send.at[self.base + slot], self.recv.at[self.base + index]
        )

    def start_far(self):
        self.far_sends(lambda one: one.start())

    def start_near(self):
        self.copy(self.line.me, self.line.far - 1, self.line.partner).start()

    def start(self):
        self.start_far()
        self.start_near()

    def relay(self, step):
        line = self.line
        handed = self.copy(self.source(step) * 2 + line.lo, line.far - 1 + step, line.partner)
        handed.wait_recv()
        if self.ends and step == 2:
            self.to_end(lambda one: one.start())
        handed.start()

    def relays(self):
        for step in range(1, self.line.far):
            self.relay(step)

    def close(self):
        line = self.line
        for step in range(line.far):
            self.copy(line.at(-step) * 2 + (1 - line.lo), 0, line.partner).wait_recv()

    def drain(self):
        self.far_sends(lambda one: one.wait_send())
        if self.ends:
            self.to_end(lambda one: one.wait_send())
        for slot in range(self.line.far - 1, 2 * self.line.far - 1):
            self.copy(self.line.me, slot, self.line.partner).wait_send()


class SideGather(Gather):
    def other(self, act):
        line = self.line
        for step in range(1, line.far):
            one = self.copy(line.partner, line.far - 1 + step, line.at(step) * 2 + line.lo)
            if self.ends and step != 2:
                pl.when(line.hi != (3 if step == 1 else 0))(functools.partial(act, one))
            else:
                act(one)

    def to_ends(self, parity, slot, act):
        line = self.line
        dest = jnp.where(line.hi == 1, 0, 3)
        one = self.copy((3 - dest) * 2 + parity, slot, dest * 2 + line.lo)
        pl.when((line.hi == 1) | (line.hi == 2))(functools.partial(act, one))

    def start_other(self):
        self.copy(self.line.partner, 0, self.line.partner).wait_recv()
        self.other(lambda one: one.start())

    def taken(self, step):
        line = self.line
        for parity, slot in ((line.lo, 2 * line.far - 1), (1 - line.lo, 2 * line.far)):
            self.copy(self.source(step) * 2 + parity, 0, line.partner).wait_recv()
            if self.ends and step == 2:
                self.to_ends(parity, slot, lambda one: one.start())

    def forward(self):
        if self.line.far > 2:
            self.taken(2)

    def close(self):
        for step in range(1, self.line.far):
            if step != 2:
                self.taken(step)

    def drain(self):
        line = self.line
        self.far_sends(lambda one: one.wait_send())
        self.copy(line.me, line.far - 1, line.partner).wait_send()
        self.other(lambda one: one.wait_send())
        if self.ends:
            for parity, slot in ((line.lo, 2 * line.far - 1), (1 - line.lo, 2 * line.far)):
                self.to_ends(parity, slot, lambda one: one.wait_send())


class SideScatter:
    def __init__(self, line, part, second, first, send, recv):
        self.line, self.part, self.second, self.first = line, part, second, first
        self.send, self.recv = send, recv

    def far_copy(self, step, parity):
        line = self.line
        hi = line.at(step)
        return line.push(
            hi * 2 + line.lo,
            self.part(hi * 2 + parity),
            self.second(parity * line.far + line.hi),
            self.send.at[2 * (step - 1) + parity],
            self.recv.at[parity * line.far + line.hi],
        )

    def near_copy(self):
        line = self.line
        return line.push(
            line.partner,
            self.part(line.partner),
            self.first,
            self.send.at[2 * line.far - 2],
            self.recv.at[2 * line.far],
        )

    def start(self):
        for step in range(1, self.line.far):
            for parity in range(2):
                self.far_copy(step, parity).start()

    def sum_of(self, parity):
        line = self.line
        value = self.part(line.hi * 2 + parity)[...].astype(F32)
        for step in range(1, line.far):
            index = parity * line.far + line.at(-step)
            block = self.second(index)
            line.push(
                line.partner, block, block, self.send.at[0], self.recv.at[index]
            ).wait_recv()
            value = value + block[...].astype(F32)
        return value

    def trade(self):
        given = self.part(self.line.partner)
        given[...] = self.sum_of(1 - self.line.lo).astype(LOW)
        self.near_copy().start()

    def arrive(self):
        pass

    def total(self):
        value = self.sum_of(self.line.lo)
        self.near_copy().wait_recv()
        return value + self.first[...].astype(F32)

    def drain(self):
        for step in range(1, self.line.far):
            for parity in range(2):
                self.far_copy(step, parity).wait_send()
        self.near_copy().wait_send()


class Scatter:
    def __init__(self, line, part, first, second, send, recv, base=0, extra=None):
        self.line, self.part, self.first, self.second = line, part, first, second
        self.send, self.recv, self.base = send, recv, base
        self.extra = extra if line.far == 4 else None

    def clear(self):
        line = self.line
        if self.extra is not None:

            @pl.when((line.hi == 0) | (line.hi == 3))
            def _():
                slot = self.second(3 - line.hi)
                slot[...] = jnp.zeros(slot.shape, LOW)

    def order(self, step):
        line = self.line
        if self.extra is None:
            return line.at(step)
        table = ((3, 2, 1), (2, 0, 3), (1, 3, 0), (0, 1, 2))
        hi = table[3][step - 1]
        for place in (2, 1, 0):
            hi = jnp.where(line.hi == place, table[place][step - 1], hi)
        return hi

    def traded(self, hi):
        line = self.line
        return line.push(
            line.partner,
            self.part(hi * 2 + (1 - line.lo)),
            self.first(hi),
            self.send.at[self.base + hi],
            self.recv.at[self.base + hi],
        )

    def passed(self, step):
        line = self.line
        hi = self.order(step)
        return line.push(
            hi * 2 + line.lo,
            self.part(hi * 2 + line.lo),
            self.second(line.hi),
            self.send.at[self.base + line.far + step - 1],
            self.recv.at[self.base + line.far + line.hi],
        )

    def to_next(self):
        line = self.line
        return line.push(
            jnp.where(line.hi < 2, 1, 2) * 2 + line.lo,
            self.part((3 - jnp.where(line.hi < 2, 0, 3)) * 2 + line.lo),
            self.extra,
            self.send.at[self.base + line.far],
            self.recv.at[self.base + 2 * line.far],
        )

    def turn_of(self, turn):
        line = self.line
        if self.extra is None:
            return lax.rem(line.hi + turn + 1, line.far)
        hi = line.hi
        for step in range(1, line.far):
            hi = jnp.where(turn == step - 1, self.order(step), hi)
        return hi

    def is_end(self):
        return (self.line.hi == 0) | (self.line.hi == 3)

    def trade(self, hi):
        self.traded(hi).start()

    def trade_all(self):
        for step in range(1, self.line.far + 1):
            self.trade(self.order(step) if step < self.line.far else self.line.hi)

    def pass_on(self, step):
        line = self.line
        hi = self.order(step)
        self.traded(hi).wait_recv()
        mine, other = self.part(hi * 2 + line.lo), self.first(hi)
        if self.extra is None or step == 2:
            mine[...] = (mine[...].astype(F32) + other[...].astype(F32)).astype(LOW)
            self.passed(step).start()
        elif step == 1:
            mine[...] = (mine[...].astype(F32) + other[...].astype(F32)).astype(LOW)

            @pl.when(self.is_end())
            def _():
                self.to_next().start()

            @pl.when(jnp.logical_not(self.is_end()))
            def _():
                self.passed(step).start()
        else:

            @pl.when(self.is_end())
            def _():
                mine[...] = (mine[...].astype(F32) + other[...].astype(F32)).astype(LOW)

            @pl.when(jnp.logical_not(self.is_end()))
            def _():
                line.push(
                    line.partner,
                    self.extra,
                    self.extra,
                    self.send.at[self.base],
                    self.recv.at[self.base + 2 * line.far],
                ).wait_recv()
                mine[...] = (
                    mine[...].astype(F32) + other[...].astype(F32) + self.extra[...].astype(F32)
                ).astype(LOW)

            self.passed(step).start()

    def arrive(self):
        line = self.line
        self.traded(line.hi).wait_recv()
        for step in range(1, line.far):
            hi = line.at(-step)
            one = line.push(
                line.partner,
                self.second(hi),
                self.second(hi),
                self.send.at[self.base],
                self.recv.at[self.base + line.far + hi],
            )
            if self.extra is None:
                one.wait_recv()
            else:
                pl.when(jnp.logical_not(self.is_end()) | (hi + line.hi != 3))(one.wait_recv)

    def total(self, here):
        line = self.line
        value = self.part(line.me)[here, :].astype(F32) + self.first(line.hi)[here, :].astype(F32)
        for step in range(1, line.far):
            value = value + self.second(line.at(-step))[here, :].astype(F32)
        return value

    def drain(self):
        line = self.line
        for step in range(line.far):
            self.traded(line.at(step)).wait_send()
        for step in range(1, line.far):
            if self.extra is not None and step == 1:
                pl.when(self.is_end())(lambda: self.to_next().wait_send())
                pl.when(jnp.logical_not(self.is_end()))(lambda: self.passed(1).wait_send())
            else:
                self.passed(step).wait_send()


def block_rows(ref, rows, first=0):
    return lambda index: ref.at[pl.ds(pl.multiple_of((index + first) * rows, rows), rows)]


def part_rows(ref, rows, first, count):
    return lambda index: ref.at[pl.ds(pl.multiple_of(index * rows + first, count), count)]


def of_index(ref):
    return lambda index: ref.at[index]


def norm_rows(values):
    center = values - jnp.mean(values, -1, keepdims=True)
    spread = jnp.mean(center * center, -1, keepdims=True)
    inverse = lax.rsqrt(spread + EPS_LAYER)
    return center * inverse, inverse


def norm_back(values, gain, grad):
    unit, inverse = norm_rows(values)
    inner = grad * gain
    shared = jnp.mean(inner, -1, keepdims=True)
    along = jnp.mean(inner * unit, -1, keepdims=True)
    return inverse * (inner - shared - unit * along), unit


def head_masks(width):
    lane = lax.broadcasted_iota(jnp.int32, (1, width), 1)
    return [
        jnp.where((lane >= head * HD) & (lane < (head + 1) * HD), 1.0, 0.0)
        for head in range(width // HD)
    ]


def spread_heads(values, masks):
    return jnp.concatenate([values * mask.astype(LOW) for mask in masks], 0)


def join_heads(values, masks, rows):
    total = values[0:rows] * masks[0]
    for head in range(1, len(masks)):
        total = total + values[head * rows : (head + 1) * rows] * masks[head]
    return total


TAIL = (
    0.2256758632450557,
    0.22566952478278277,
    0.2078438574180613,
    0.16853390514724884,
    0.14146086231844687,
    -0.005667717379728321,
    0.16915486959066833,
    -0.18294364197603524,
    0.05027260226320005,
)


def normal_tail(size, bell):
    base = 1.0 + (0.4 * 0.5**0.5) * size
    t = pl.reciprocal(base, approx=True)
    t = t * (2.0 - base * t)
    t = t * (2.0 - base * t)
    value = jnp.full_like(t, 0.5 * TAIL[-1])
    for factor in TAIL[-2::-1]:
        value = value * t + 0.5 * factor
    return value * t * bell


def far_copies(line, make, sends, recvs):
    def copy(step):
        dest = lax.rem(line.me + step, line.size)
        src, dst = make(dest, line.me)
        return line.push(dest, src, dst, sends.at[step], recvs.at[line.me])

    def wait():
        for step in range(1, line.size):
            source = lax.rem(line.me + line.size - step, line.size)
            _, dst = make(source, source)
            line.push(line.partner, dst, dst, sends.at[0], recvs.at[source]).wait_recv()

    return copy, wait


def layer_kernel(cap, names, *refs):
    R = types.SimpleNamespace(**dict(zip(names, refs)))
    dp, mp = Line("dp"), Line("mp")
    size, ways = dp.size, mp.size
    seqs, seq_len = R.ids.shape
    tokens, width = R.noise.shape
    model = R.cot.shape[1]
    heads_w = R.o.shape[1]
    hidden = R.wbf.shape[1]
    table_rows = R.table.shape[0]
    rin = R.w_in.shape[0]
    rin_up = round_up(rin, 16)
    quarter = model // ways
    strip = R.w_up.shape[0]
    spots = size * cap
    far = mp.far
    count = seqs * far
    half_strip = strip // 2
    own_strip = pl.ds(pl.multiple_of(dp.me * strip, strip), strip)
    mine = pl.ds(pl.multiple_of(dp.me * cap, cap), cap)

    some_rows = seq_len // 2

    def rows_of(piece):
        return lambda row: pl.ds(pl.multiple_of(piece * seq_len + row, some_rows), some_rows)

    def own_rows(piece):
        first = pl.multiple_of((piece * ways + mp.me) * seq_len, seq_len)
        return lambda row: pl.ds(pl.multiple_of(first + row, some_rows), some_rows)

    def by_rows(body, after=lambda half: None):
        for half in range(2):
            body(half * some_rows)
            after(half)

    class Rows:
        def __init__(self, ref, send, recv, piece):
            self.parts = [
                Gather(
                    mp,
                    lambda index, half=half: ref.at[
                        pl.ds(
                            pl.multiple_of(
                                (piece * ways + index) * seq_len + half * some_rows, some_rows
                            ),
                            some_rows,
                        )
                    ],
                    send,
                    recv,
                    (2 * piece + half) * ways,
                )
                for half in range(2)
            ]

        def start(self, half):
            self.parts[half].start()

        def relays(self):
            for part in self.parts:
                part.relays()

        def close(self):
            for part in self.parts:
                part.close()

        def drain(self):
            for part in self.parts:
                part.drain()

    def halves(ref, send, recv):
        return [Rows(ref, send, recv, piece) for piece in range(seqs)]

    chunk_cols = min(256, model)
    chunk_count = model // chunk_cols

    class Sums:
        def __init__(self, *refs):
            *self.refs, self.send, self.recv = refs

        def chunk(self, piece, chunk):
            cols = pl.ds(pl.multiple_of(chunk * chunk_cols, chunk_cols), chunk_cols)

            def blocks(ref, first):
                return lambda index: ref.at[
                    pl.ds(pl.multiple_of((index + first) * seq_len, seq_len), seq_len), cols
                ]

            firsts = (piece * ways, piece * far, piece * far)
            views = [blocks(ref, first) for ref, first in zip(self.refs, firsts)]
            return Scatter(mp, *views, self.send, self.recv, (piece * chunk_count + chunk) * ways)

        def total(self, piece, here):
            firsts = (piece * ways, piece * far, piece * far)
            views = [block_rows(ref, seq_len, first) for ref, first in zip(self.refs, firsts)]
            return Scatter(mp, *views, self.send, self.recv).total(here)

        def trade(self, piece, chunk):
            self.chunk(piece, chunk).trade_all()

        def hand_on(self, piece, chunk):
            scatter = self.chunk(piece, chunk)
            for step in range(1, far):
                scatter.pass_on(step)

        def every(self, act):
            def one(chunk, carry):
                act(chunk)
                return carry

            lax.fori_loop(0, chunk_count, one, 0)

        def hand_on_all(self, piece):
            self.every(lambda chunk: self.hand_on(piece, chunk))

        def arrive(self, piece):
            self.every(lambda chunk: self.chunk(piece, chunk).arrive())

        def drain(self, piece):
            self.every(lambda chunk: self.chunk(piece, chunk).drain())

        def products(self, piece, make):
            def one(chunk, carry):
                make(pl.ds(pl.multiple_of(chunk * chunk_cols, chunk_cols), chunk_cols))
                self.trade(piece, chunk)
                pl.when(chunk > 0)(lambda: self.hand_on(piece, chunk - 1))
                return carry

            lax.fori_loop(0, chunk_count, one, 0)

        def hand_on_last(self, piece):
            self.hand_on(piece, chunk_count - 1)

    many = ways * seq_len

    def turns(body, hooks=()):
        def one(piece, carry):
            def at(point):
                for place, when, action in hooks:
                    if when == point:
                        pl.when(piece == place)(action)

            base = pl.multiple_of(piece * many, many)
            body(piece, base, pl.ds(base, many), at)
            return carry

        lax.fori_loop(0, seqs, one, 0)

    def pairs(base, body):
        def one(pair, carry):
            first = pl.multiple_of(base + pair * (2 * seq_len), 2 * seq_len)
            body([pl.ds(pl.multiple_of(first + seq * seq_len, seq_len), seq_len) for seq in range(2)])
            return carry

        lax.fori_loop(0, far, one, 0)

    def chunks(total, body):
        step = min(256, total)
        lax.fori_loop(
            0,
            total // step,
            lambda turn, carry: (body(pl.ds(pl.multiple_of(turn * step, step), step)), carry)[1],
            0,
        )

    def later_pieces(gathers, point):
        hooks = []
        for piece in range(1, seqs):
            hooks.append((piece - 1, point, gathers[piece].relays))
            hooks.append((piece, "start", gathers[piece].close))
        return hooks

    chunk = R.tab.shape[1]
    pieces = -(-table_rows // chunk)

    def fetch(piece):
        rows = min(chunk, table_rows - piece * chunk)
        return pltpu.make_async_copy(
            R.table.at[pl.ds(piece * chunk, rows)],
            R.tab.at[piece % 2, pl.ds(0, rows)],
            R.tab_sem.at[piece % 2],
        )

    for piece in range(min(2, pieces)):
        fetch(piece).start()

    names_of_moments = [
        name + kind for name in ("w_in", "ln", "qkv", "out", "up", "down") for kind in ("_m", "_v")
    ]

    def moment(name):
        return pltpu.make_async_copy(
            getattr(R, name), getattr(R, name + "_here"), R.moment_sem.at[names_of_moments.index(name)]
        )

    tile_rows = R.tw.shape[1]
    tiles = table_rows // tile_rows

    shares_of = -(-tiles // ways)

    def share_tile(turn):
        return lax.min(turn * ways + mp.me, tiles - 1)

    def tile_of(turn):
        side = lax.rem(turn, 2)
        rows = pl.ds(pl.multiple_of(share_tile(turn) * tile_rows, tile_rows), tile_rows)
        return [
            pltpu.make_async_copy(source.at[rows], dest.at[side], R.tile_sem.at[2 * place + side])
            for place, (source, dest) in enumerate(
                ((R.table, R.tw), (R.table_m, R.tm), (R.table_v, R.tv))
            )
        ]

    eye = lax.broadcasted_iota(jnp.int32, (seq_len, seq_len), 0) == lax.broadcasted_iota(
        jnp.int32, (seq_len, seq_len), 1
    )
    id_rows = R.ids[...].astype(F32)
    ids = jnp.concatenate(
        [
            jnp.sum(jnp.where(eye, id_rows[seq : seq + 1, :], 0.0), 1, keepdims=True)
            for seq in range(seqs)
        ],
        0,
    )
    lane = lax.broadcasted_iota(jnp.int32, (tokens, 128), 1).astype(F32)
    low_end = lane * float(table_rows)
    owned = jnp.where((ids >= low_end) & (ids < low_end + float(table_rows)), 1.0, 0.0)
    before = jnp.where(
        lax.broadcasted_iota(jnp.int32, (tokens, tokens), 0)
        >= lax.broadcasted_iota(jnp.int32, (tokens, tokens), 1),
        1.0,
        0.0,
    )
    ranks = dot(before.astype(LOW), owned.astype(LOW))
    rank = jnp.sum(owned * ranks, 1, keepdims=True) - 1.0
    slot = jnp.sum(owned * lane, 1, keepdims=True) * cap + rank
    placed = jnp.where(lane == rank, 1.0, 0.0)
    upper = jnp.floor(ids * (1.0 / 256.0))
    lower = ids - upper * 256.0
    parts = jnp.concatenate([placed * upper, placed * lower, placed], 1).astype(LOW)
    asked = dot_tn(owned.astype(LOW), parts)
    asked = asked[:, :128] * 256.0 + asked[:, 128:256] + asked[:, 256:] - 1.0
    wide_ln = R.ln_params.shape[1]
    shares = R.ln_params[...].astype(LOW).astype(F32)
    if wide_ln < 128:
        shares = jnp.concatenate([shares, jnp.zeros((4, 128 - wide_ln), F32)], 1)
    for index in range(size):
        R.ask[index] = jnp.concatenate(
            [asked[index : index + 1, :], shares, jnp.zeros((3, 128), F32)], 0
        )
    R.idx[mp.me, dp.me] = R.ask[dp.me]

    def spread(part, first, second, extra, send, recv):
        blocks = [block_rows(ref, strip) for ref in (part, first, second)]
        return Scatter(dp, *blocks, send, recv, 0, extra)

    up = spread(R.wbf, R.up_first, R.up_second, R.up_extra, R.up_send, R.up_recv)
    down = spread(R.gdn, R.dn_first, R.dn_second, R.dn_extra, R.dn_send, R.dn_recv)
    first_w = spread(
        R.waf.at[:, : 3 * heads_w], R.wa_first, R.wa_second, R.wa_extra, R.ga_send, R.ga_recv
    )
    wo = SideScatter(
        dp,
        *[block_rows(ref, strip) for ref in (R.gwo, R.wo_second)],
        R.wo_first,
        R.wo_send,
        R.wo_recv,
    )
    small = Scatter(
        dp,
        *[of_index(ref) for ref in (R.gw, R.gw_first, R.gw_second)],
        R.gw_send,
        R.gw_recv,
        0,
        R.gw_extra,
    )
    for scatter in (up, down, first_w, small):
        scatter.clear()

    meet([mp], [dp])
    ask, ask_wait = far_copies(
        dp,
        lambda dest, source: (R.ask.at[dest], R.idx.at[mp.me, source]),
        R.ask_send,
        R.ask_recv,
    )
    for step in range(1, size):
        ask(step).start()

    mine_in = R.winf.at[mp.me]
    win = Gather(dp, block_rows(mine_in, rin), R.win_send, R.win_recv, 0, True)
    win_all = Gather(mp, of_index(R.winf), R.wim_send, R.wim_recv)
    wa = [
        Gather(dp, part_rows(R.waf, strip, piece * half_strip, half_strip), send, recv, 0, True)
        for piece, (send, recv) in enumerate(((R.wa_send, R.wa_recv), (R.wx_send, R.wx_recv)))
    ]
    wb = Gather(dp, block_rows(R.wbf, strip), R.wb_send, R.wb_recv, 0, True)
    wc = Gather(dp, part_rows(R.wcf, strip, 0, half_strip), R.wc_send, R.wc_recv, 0, True)
    wd = SideGather(dp, part_rows(R.wcf, strip, half_strip, half_strip), R.wd_send, R.wd_recv, 0, True)
    dxg = Gather(
        mp,
        lambda index: R.dx.at[:, pl.ds(pl.multiple_of(index * seq_len, seq_len), seq_len)],
        R.dx_send,
        R.dx_recv,
    )
    ag = halves(R.a, R.a_send, R.a_recv)
    cg = halves(R.c, R.c_send, R.c_recv)
    mg = halves(R.dmid_all, R.e_send, R.e_recv)

    mine_in[pl.ds(pl.multiple_of(dp.me * rin, rin), rin), :] = (
        R.w_in[:, pl.ds(pl.multiple_of(mp.me * quarter, quarter), quarter)]
        .astype(LOW)
        .astype(R.winf.dtype)
    )
    win.start()
    for part in range(3):
        R.waf[own_strip, part * heads_w : (part + 1) * heads_w] = R.w_qkv[part].astype(LOW)
    R.waf[own_strip, 3 * heads_w :] = R.w_out[...].T.astype(LOW)
    wa[0].start()
    wa[1].start_near()
    for name in names_of_moments:
        moment(name).start()

    win.relays()

    ask_wait()
    small_eye = lax.broadcasted_iota(jnp.int32, (cap, 128), 0) == lax.broadcasted_iota(
        jnp.int32, (cap, 128), 1
    )

    def locate(index, carry):
        row = R.idx[mp.me, index][0:1, :]
        column = jnp.sum(jnp.where(small_eye, row, 0.0), 1, keepdims=True)
        local = column.astype(jnp.int32) - dp.me * table_rows
        R.loc[pl.ds(pl.multiple_of(index * cap, cap), cap), :] = jnp.broadcast_to(local, (cap, 128))
        return carry

    lax.fori_loop(0, size, locate, 0, unroll=True)
    found = None
    for piece in range(pieces):
        fetch(piece).wait()
        rows = min(chunk, table_rows - piece * chunk)
        if rows < chunk:
            R.tab[piece % 2, rows:, :] = jnp.zeros((chunk - rows, width), F32)
        hit = (
            lax.broadcasted_iota(jnp.int32, (spots, chunk), 1) + piece * chunk == R.loc[:, 0:1]
        )
        more = dot(jnp.where(hit, 1.0, 0.0).astype(LOW), R.tab[piece % 2].astype(LOW))
        found = more if found is None else found + more
        if piece + 2 < pieces:
            fetch(piece + 2).start()
    R.give[...] = found.astype(LOW)

    give, give_wait = far_copies(
        dp,
        lambda dest, source: (block_rows(R.give, cap)(dest), block_rows(R.got, cap)(source)),
        R.give_send,
        R.give_recv,
    )
    for step in range(1, size):
        give(step).start()
    R.got[mine, :] = R.give[mine, :]
    wa[1].start_far()
    win.close()
    win_all.start()
    wa[0].relay(1)
    for seq in range(seqs):
        level = jnp.full((seq_len, 1), R.levels[seq], jnp.int32).astype(F32) / (LEVELS - 1)
        R.sig[seq * seq_len : (seq + 1) * seq_len, :] = jnp.exp(level * jnp.log(SIGMA_TOP))

    def scale_at(here):
        sig = R.sig[here, :]
        return sig * lax.rsqrt(1.0 + sig * sig)

    for piece in range(seqs):
        here = rows_of(piece)

        def scale_cot(row, here=here, piece=piece):
            there = pl.ds(pl.multiple_of(mp.me * seq_len + row, some_rows), some_rows)
            R.dx[piece, there, :] = (R.cot[here(row), :].astype(F32) * scale_at(here(row))).astype(LOW)

        by_rows(scale_cot)
    dxg.start()
    R.wbf[own_strip, :] = R.w_up[...].astype(LOW)
    R.wcf[own_strip, :] = R.w_down[...].T.astype(LOW)
    wb.start_near()
    R.pick[...] = jnp.where(
        lax.broadcasted_iota(jnp.int32, (tokens, spots), 1).astype(F32) == slot, 1.0, 0.0
    ).astype(LOW)
    win_all.relays()
    wa[0].relay(2)
    if wide_ln % 128 == 0:
        R.gains[...] = jnp.concatenate([R.idx[mp.me, index] for index in range(size)], 1)
    else:
        total = jnp.zeros((8, model), F32)
        for index in range(size):
            place = lax.broadcasted_iota(
                jnp.int32, (128, model), 1
            ) == index * wide_ln + lax.broadcasted_iota(jnp.int32, (128, model), 0)
            place = place & (lax.broadcasted_iota(jnp.int32, (128, model), 0) < wide_ln)
            total = total + dot(
                R.idx[mp.me, index].astype(LOW), jnp.where(place, 1.0, 0.0).astype(LOW)
            )
        R.gains[...] = total
    for step in range(3, dp.far):
        wa[0].relay(step)
    named = Gather(mp, of_index(R.idx), R.id_send, R.id_recv)

    give_wait()
    rows = dot(R.pick[...], R.got[...])
    R.rows[...] = rows.astype(LOW)
    sig = R.sig[...]
    unit = rows * lax.rsqrt(jnp.mean(rows * rows, -1, keepdims=True) + EPS_NORM)
    R.mixed[...] = ((unit + sig * R.noise[...].astype(F32)) * lax.rsqrt(1.0 + sig * sig)).astype(LOW)
    win_all.close()
    for index in range(ways):
        R.x0[:, index * quarter : (index + 1) * quarter] = dot(
            R.mixed[...], R.winf[index].astype(LOW)
        )

    for piece in range(seqs):
        here, there = rows_of(piece), own_rows(piece)

        def first_norm(row, here=here, there=there):
            normed, _ = norm_rows(R.x0[here(row), :])
            R.a[there(row), :] = (normed * R.gains[1:2, :] + R.gains[2:3, :]).astype(LOW)

        by_rows(first_norm, ag[piece].start)
    wa[1].relay(1)
    wb.start_far()
    for step in range(2, dp.far):
        wa[1].relay(step)
    dxg.relays()
    ag[0].relays()
    for gather in (*wa, ag[0]):
        gather.close()

    att = Sums(R.part, R.fold, R.fold_far, R.as_send, R.as_recv)
    dcs = Sums(R.part, R.fold, R.fold_far, R.cs_send, R.cs_recv)
    das = Sums(R.part, R.fold, R.fold_far, R.ds_send, R.ds_recv)
    out = Sums(R.c, R.first, R.second, R.os_send, R.os_recv)
    masks = head_masks(heads_w)

    all_rows = (heads_w // HD) * seq_len
    scale = HD ** (-0.5)

    def softmax(seq, row):
        scores = R.scores[seq, row : row + 64, :]
        raised = jnp.exp((scores - jnp.max(scores, -1, keepdims=True)) * scale)
        return raised * (1.0 / jnp.sum(raised, -1, keepdims=True))

    def attend(piece, base, here, at):
        at("start")
        for part in range(3):
            cols = slice(part * heads_w, (part + 1) * heads_w)
            R.qkv[here, cols] = dot(R.a[here, :], R.waf[:, cols]).astype(LOW)
        at("mid")

        def one(rows_at):
            for seq, rows in enumerate(rows_at):
                queries = spread_heads(R.qkv[rows, :heads_w], masks)
                R.scores[seq] = dot_nt(queries, R.qkv[rows, heads_w : 2 * heads_w])
            for seq, rows in enumerate(rows_at):
                for row in range(0, all_rows, 64):
                    R.probs[seq, row : row + 64, :] = softmax(seq, row).astype(LOW)
                seen = dot(R.probs[seq], R.qkv[rows, 2 * heads_w : 3 * heads_w])
                R.o[rows, :] = join_heads(seen, masks, seq_len).astype(LOW)

        pairs(base, one)
        at("late")

        def project(cols):
            R.part[here, cols] = dot_nt(R.o[here, :], R.waf[cols, 3 * heads_w :]).astype(LOW)

        def one_chunk(chunk, carry):
            project(pl.ds(pl.multiple_of(chunk * chunk_cols, chunk_cols), chunk_cols))
            att.trade(piece, chunk)
            return carry

        lax.fori_loop(0, chunk_count, one_chunk, 0)

    def second_norm(piece):
        here, there = rows_of(piece), own_rows(piece)
        att.arrive(piece)

        def norm(row):
            x1 = R.x0[here(row), :] + att.total(piece, pl.ds(row, some_rows))
            R.out[here(row), :] = x1
            normed, _ = norm_rows(x1)
            R.c[there(row), :] = (normed * R.gains[3:4, :] + R.gains[4:5, :]).astype(LOW)

        by_rows(norm, cg[piece].start)

    def first_wb():
        wb.relay(1)
        wd.start_near()
        wc.start_near()
        wc.start_far()

    def middle_wb():
        wb.relay(2)
        wd.start_far()

    def last_wb():
        wd.start_other()
        for step in range(3, dp.far):
            wb.relay(step)
        named.start()

    turns(
        attend,
        [
            *later_pieces(ag, "mid"),
            *[
                (piece + 1, "mid", functools.partial(att.hand_on_all, piece))
                for piece in range(seqs - 1)
            ],
            (0, "mid", first_wb),
            (0, "late", middle_wb),
            (1, "mid", last_wb),
            *[
                (piece + 1, "late", functools.partial(second_norm, piece))
                for piece in range(seqs - 1)
            ],
        ],
    )
    att.hand_on_all(seqs - 1)
    wc.relay(1)
    for gather in (*wa, *ag, dxg, win):
        gather.drain()
    for step in range(1, size):
        ask(step).wait_send()
    second_norm(seqs - 1)
    cg[0].relays()
    wc.relay(2)
    wb.close()
    named.relays()
    cg[0].close()
    for piece in range(seqs):
        att.drain(piece)

    def activate(piece, base, here, at):
        at("start")

        def some(cols):
            R.h[...] = dot(R.c[here, :], R.wbf[:, cols])

            def gelu(row):
                there = pl.ds(pl.multiple_of(base + row, 64), 64)
                h = R.h[pl.ds(row, 64), :]
                bell = jnp.exp(-0.5 * h * h)
                tail = normal_tail(jnp.abs(h), bell)
                gate = jnp.where(h >= 0.0, 1.0 - tail, tail)
                slope = gate + h * (bell * 0.3989422804014327)
                R.hb[there, cols] = (h * gate).astype(LOW)
                R.slope[there, cols] = slope.astype(LOW)

            strips(many, 64, gelu, 2)

        chunks(hidden, some)
        at("end")

    def last_wc():
        for step in range(3, dp.far):
            wc.relay(step)

    turns(activate, [*later_pieces(cg, "end"), (0, "end", last_wc), (seqs - 1, "start", wd.forward)])

    due = [(scatter, step) for scatter in (down, up) for step in range(1, dp.far)]

    def pass_due(number):
        for _ in range(min(number, len(due))):
            scatter, step = due.pop(0)
            scatter.pass_on(step)

    block = 2 * strip if (2 * strip) % 128 == 0 else min(256, model)

    def grads(make, trades):
        if block == 2 * strip:

            def turn_of(turn, carry):
                hi = up.turn_of(turn)
                make(pl.ds(pl.multiple_of(hi * block, block), block))
                for scatter in trades:
                    scatter.trade(hi)
                return carry

            lax.fori_loop(0, dp.far, turn_of, 0)
        else:
            strips(model, block, lambda col: make(pl.ds(col, block)))
            for scatter in trades:
                scatter.trade_all()

    def down_grads(cols):
        every = R.dx[:, :, cols]
        R.gdn[cols, :] = dot_tn(every.reshape(seqs * many, block), R.hb[...]).astype(LOW)

    def up_grads(cols):
        R.wbf[cols, :] = dot_tn(R.c[:, cols], R.dhb[...]).astype(LOW)

    dxg.close()
    grads(down_grads, (down,))
    named.close()
    groups = ways * size
    some, lanes_at = min(groups, 32), min(ways * spots, 512)
    for begin in range(0, ways * spots, lanes_at):
        spot = lax.broadcasted_iota(jnp.int32, (128, lanes_at), 1).astype(F32) + float(begin)
        block_no = jnp.floor((spot + 0.5) * (1.0 / cap))
        place = lax.broadcasted_iota(jnp.int32, (128, lanes_at), 0).astype(F32)
        spread_out = jnp.where(spot - block_no * cap == place, 1.0, 0.0).astype(LOW)
        named_row = jnp.zeros((1, lanes_at), F32)
        for first in range(0, groups, some):
            wanted = jnp.concatenate(
                [
                    R.idx[index // size, index % size][0:1, :] + 1.0
                    for index in range(first, first + some)
                ],
                0,
            )
            high = jnp.floor(wanted * (1.0 / 256.0))
            rest = wanted - 256.0 * high
            laid = dot(high.astype(LOW), spread_out) * 256.0 + dot(rest.astype(LOW), spread_out) - 1.0
            own_block = block_no[0:1, :] == float(first) + lax.broadcasted_iota(
                jnp.int32, (some, lanes_at), 0
            ).astype(F32)
            named_row = named_row + jnp.sum(jnp.where(own_block, laid, 0.0), 0, keepdims=True)
        R.named[:, begin : begin + lanes_at] = jnp.broadcast_to(
            named_row.astype(jnp.int32) - dp.me * table_rows, (8, lanes_at)
        )
    named.drain()
    wc.close()
    wd.close()
    for gather in (wb, *cg):
        gather.drain()

    def feed_back(piece, base, here, at):
        at("start")

        def some(cols):
            bent = dot(R.dx[piece], R.wcf[:, cols]) * R.slope[here, cols].astype(F32)
            R.dhb[here, cols] = bent.astype(LOW)

        chunks(hidden, some)
        at("mid")

        def project(cols):
            R.part[here, cols] = dot_nt(R.dhb[here, :], R.wbf[cols, :]).astype(LOW)

        dcs.products(piece, project)

    R.norms[...] = jnp.zeros_like(R.norms)

    def second_back(piece):
        here, there = rows_of(piece), own_rows(piece)
        dcs.arrive(piece)

        def back(row):
            dc = dcs.total(piece, pl.ds(row, some_rows))
            grad, unit = norm_back(R.out[here(row), :], R.gains[3:4, :], dc)
            grad = grad + R.cot[here(row), :].astype(F32) * scale_at(here(row))
            R.dmid[here(row), :] = grad
            R.dmid_all[there(row), :] = grad.astype(LOW)
            R.norms[2:3, :] += jnp.sum(dc * unit, 0, keepdims=True)
            R.norms[3:4, :] += jnp.sum(dc, 0, keepdims=True)

        by_rows(back, mg[piece].start)

    turns(
        feed_back,
        [
            *[
                (piece + 1, "mid", functools.partial(dcs.hand_on_last, piece))
                for piece in range(seqs - 1)
            ],
            (1, "mid", lambda: pass_due(1)),
        ],
    )
    dcs.hand_on_last(seqs - 1)
    second_back(0)
    pass_due(1)
    grads(up_grads, (up,))
    for piece in range(1, seqs):
        second_back(piece)
    pass_due(max(1, dp.far - 3))
    mg[0].relays()
    mg[0].close()
    for piece in range(seqs):
        dcs.drain(piece)

    def attend_back(piece, base, here, at):
        at("start")
        R.low[...] = dot(R.dmid_all[here, :], R.waf[:, 3 * heads_w :]).astype(LOW)
        at("mid")

        def one(rows_at):
            for seq, rows in enumerate(rows_at):
                queries = spread_heads(R.qkv[rows, :heads_w], masks)
                R.scores[seq] = dot_nt(queries, R.qkv[rows, heads_w : 2 * heads_w])
                upper_rows = pl.ds(pl.multiple_of(rows.start - base, seq_len), seq_len)
                R.upper[seq] = spread_heads(R.low[upper_rows, :], masks)
                R.dprobs[seq] = dot_nt(R.upper[seq], R.qkv[rows, 2 * heads_w : 3 * heads_w])
            for seq, rows in enumerate(rows_at):
                for row in range(0, all_rows, 64):
                    probs = softmax(seq, row)
                    grad_probs = R.dprobs[seq, row : row + 64, :]
                    inner = jnp.sum(probs * grad_probs, -1, keepdims=True)
                    R.probs[seq, row : row + 64, :] = probs.astype(LOW)
                    R.dscores[seq, row : row + 64, :] = (probs * (grad_probs - inner)).astype(LOW)
                keys = R.qkv[rows, heads_w : 2 * heads_w]
                queries = spread_heads(R.qkv[rows, :heads_w], masks)
                R.qkv[rows, 2 * heads_w : 3 * heads_w] = dot_tn(R.probs[seq], R.upper[seq]).astype(LOW)
                R.qkv[rows, heads_w : 2 * heads_w] = (dot_tn(R.dscores[seq], queries) * scale).astype(
                    LOW
                )
                R.qkv[rows, :heads_w] = (
                    join_heads(dot(R.dscores[seq], keys), masks, seq_len) * scale
                ).astype(LOW)

        pairs(base, one)
        at("late")

        def project(cols):
            R.part[here, cols] = dot_nt(R.qkv[here, :], R.waf[cols, : 3 * heads_w]).astype(LOW)

        das.products(piece, project)

    def first_back(piece):
        here = rows_of(piece)
        das.arrive(piece)

        def back(row):
            da = das.total(piece, pl.ds(row, some_rows))
            grad, unit = norm_back(R.x0[here(row), :], R.gains[1:2, :], da)
            R.dx0[here(row), :] = (R.dmid[here(row), :] + grad).astype(LOW)
            R.norms[0:1, :] += jnp.sum(da * unit, 0, keepdims=True)
            R.norms[1:2, :] += jnp.sum(da, 0, keepdims=True)

        by_rows(back)

    def out_grads():
        def make(cols):
            R.gwo[cols, :] = dot_tn(R.dmid_all[:, cols], R.o[...]).astype(LOW)

        grads(make, (wo,))

    turns(
        attend_back,
        [
            *later_pieces(mg, "mid"),
            (0, "late", lambda: pass_due(1)),
            *[
                (piece + 1, "mid", functools.partial(das.hand_on_last, piece))
                for piece in range(seqs - 1)
            ],
            (seqs - 1, "late", lambda: pass_due(1)),
        ],
    )
    das.hand_on_last(seqs - 1)
    def out_grads(cols):
        R.gwo[cols, :] = dot_tn(R.dmid_all[:, cols], R.o[...]).astype(LOW)

    def attend_grads(cols):
        R.waf[cols, : 3 * heads_w] = dot_tn(R.a[:, cols], R.qkv[...]).astype(LOW)

    grads(out_grads, ())
    wo.start()
    first_back(0)
    grads(attend_grads, (first_w,))
    for piece in range(1, seqs):
        first_back(piece)

    grad_mixed = sum(
        dot_nt(R.dx0[:, index * quarter : (index + 1) * quarter], R.winf[index].astype(LOW))
        for index in range(ways)
    )
    sig = R.sig[...]
    grad_unit = grad_mixed * lax.rsqrt(1.0 + sig * sig)
    rows = R.rows[...].astype(F32)
    inverse = lax.rsqrt(jnp.mean(rows * rows, -1, keepdims=True) + EPS_NORM)
    unit = rows * inverse
    grad_rows = inverse * (grad_unit - unit * jnp.mean(grad_unit * unit, -1, keepdims=True))
    for step in range(1, size):
        give(step).wait_send()
    R.give[...] = dot_tn(R.pick[...], grad_rows.astype(LOW)).astype(LOW)
    mine_inc = block_rows(R.inc, spots)(mp.me)
    back, back_wait = far_copies(
        dp,
        lambda dest, source: (block_rows(R.give, cap)(dest), block_rows(mine_inc, cap)(source)),
        R.back_send,
        R.back_recv,
    )
    for step in range(1, size):
        back(step).start()
    mine_inc[mine, :] = R.give[mine, :]

    small_mp = Scatter(
        mp, of_index(R.gm), of_index(R.gm_first), of_index(R.gm_second), R.gm_send, R.gm_recv
    )
    for index in range(ways):
        cols = slice(index * quarter, (index + 1) * quarter)
        R.gm[index, :width, :] = dot_tn(R.mixed[...], R.dx0[:, cols]).astype(LOW)
        R.gm[index, width:, :] = jnp.concatenate(
            [R.norms[0:4, cols], jnp.zeros((12, quarter), F32)], 0
        ).astype(LOW)
    small_mp.trade_all()
    pass_due(len(due))
    for step in range(1, far):
        small_mp.pass_on(step)

    first_w.pass_on(1)

    def feed_out(piece, base, here, at):
        def project(cols):
            R.c[here, cols] = dot_nt(R.hb[here, :], R.wcf[cols, :]).astype(LOW)

        out.products(piece, project)

    turns(feed_out)
    wo.trade()
    first_w.pass_on(2)
    for turn in range(min(2, shares_of)):
        for one in tile_of(turn):
            one.start()
    back_wait()
    rows_in = Gather(mp, block_rows(R.inc, spots), R.in_send, R.in_recv)
    rows_in.start()
    for piece in range(seqs):
        out.hand_on_last(piece)

    small_mp.arrive()
    summed = small_mp.total(slice(None))
    for index in range(size):
        piece = summed[index * rin : (index + 1) * rin, :]
        if rin_up > rin:
            piece = jnp.concatenate([piece, jnp.zeros((rin_up - rin, quarter), F32)], 0)
        R.gw[index, :rin_up, :] = piece.astype(LOW)
        R.gw[index, rin_up:, :] = summed[width:, :].astype(LOW)
    small.trade_all()
    rows_in.relays()
    for step in range(3, dp.far):
        first_w.pass_on(step)

    def finish_out(piece):
        here = rows_of(piece)
        out.arrive(piece)

        def finish(row):
            R.out[here(row), :] = (
                R.out[here(row), :] + out.total(piece, pl.ds(row, some_rows))
            ) * scale_at(here(row))

        by_rows(finish)

    for piece in range(seqs):
        finish_out(piece)

    rows_in.close()

    once = jnp.where(mp.me == 0, 1.0, 0.0)
    lanes = lax.broadcasted_iota(jnp.int32, (1, 128), 1)
    R.sums[...] = jnp.zeros_like(R.sums)

    def put(place, squares, factor=None):
        for row, values in enumerate(squares):
            total = jnp.sum(jnp.sum(values, 0, keepdims=True), 1, keepdims=True)
            if factor is not None:
                total = total * factor
            R.sums[row : row + 1, :] += jnp.where(lanes == place, total, 0.0)

    def squares_of(weight, gradient, first, second):
        direction = direction_of(weight, gradient, first, second)[2]
        return weight * weight, direction * direction

    def folded(values):
        rows, columns = values.shape
        return jnp.sum(values.reshape(rows // 8, 8, columns), 0)

    def add_up(weight, gradient, first, second):
        squares = squares_of(weight[...], gradient[...], first[...], second[...])
        return [folded(values) for values in squares]

    zero = jnp.zeros((8, width), F32)

    rest = [
        functools.partial(scatter.pass_on, step)
        for scatter in (small,)
        for step in range(1, dp.far)
    ]
    tail_hooks = [
        (min(shares_of - 1, place * shares_of // len(rest)), action)
        for place, action in enumerate(rest)
    ]

    def add_tile(turn, carry):
        side = lax.rem(turn, 2)
        for place, action in tail_hooks:
            pl.when(turn == place)(action)
        for one in tile_of(turn):
            one.wait()
        hit = (
            lax.broadcasted_iota(jnp.int32, (tile_rows, ways * spots), 0)
            + share_tile(turn) * tile_rows
            == R.named[0:1, :]
        )
        gradient = dot(jnp.where(hit, 1.0, 0.0).astype(LOW), R.inc[...])
        more = add_up(R.tw.at[side], gradient, R.tm.at[side], R.tv.at[side])
        counts = jnp.where(turn * ways + mp.me < tiles, 1.0, 0.0)

        @pl.when(turn + 2 < shares_of)
        def _():
            for one in tile_of(turn + 2):
                one.start()

        return carry[0] + counts * more[0], carry[1] + counts * more[1]

    put(0, lax.fori_loop(0, shares_of, add_tile, (zero, zero)))

    for thing in (win_all, wc, wd, *mg, up, down, small_mp):
        thing.drain()
    for piece in range(seqs):
        out.drain(piece)
        das.drain(piece)
    for step in range(1, size):
        back(step).wait_send()

    for name in names_of_moments:
        moment(name).wait()
    up.arrive()

    R.red_up[...] = up.total(slice(None))
    put(10, add_up(R.w_up, R.red_up, R.up_m_here, R.up_v_here))
    down.arrive()

    R.red_dn[...] = down.total(slice(None)).T
    put(11, add_up(R.w_down, R.red_dn, R.down_m_here, R.down_v_here))
    wo.arrive()
    R.red_out[...] = wo.total().T
    put(9, add_up(R.w_out, R.red_out, R.out_m_here, R.out_v_here))

    small.arrive()
    R.wsum[mp.me] = small.total(slice(None)).astype(LOW)
    weights_in = Gather(mp, of_index(R.wsum), R.ws_send, R.ws_recv)
    weights_in.start()
    first_w.arrive()

    value = first_w.total(slice(None))
    for part in range(3):
        R.red_qkv[part] = value[:, part * heads_w : (part + 1) * heads_w]
    weights_in.relays()
    for part in range(3):
        put(
            6 + part,
            add_up(
                R.w_qkv.at[part], R.red_qkv.at[part], R.qkv_m_here.at[part], R.qkv_v_here.at[part]
            ),
        )
    weights_in.close()
    total = jnp.concatenate([R.wsum[index].astype(F32) for index in range(ways)], 1)
    R.red_in[...] = total[:rin, :]
    put(1, add_up(R.w_in, R.red_in, R.w_in_m_here, R.w_in_v_here), once)
    if strip % 128 == 0:
        R.lnsum[...] = total[rin_up : rin_up + 8, :]
        R.red_ln[...] = R.lnsum[0:4, pl.ds(pl.multiple_of(dp.me * strip, strip), strip)]
    else:
        chosen = lax.broadcasted_iota(jnp.int32, (model, strip), 0) == dp.me * strip + (
            lax.broadcasted_iota(jnp.int32, (model, strip), 1)
        )
        R.red_ln[...] = dot(
            total[rin_up : rin_up + 8, :].astype(LOW), jnp.where(chosen, 1.0, 0.0).astype(LOW)
        )[0:4]
    squares = squares_of(R.ln_params[...], R.red_ln[...], R.ln_m_here[...], R.ln_v_here[...])
    for row in range(4):
        put(2 + row, [values[row : row + 1, :] for values in squares], once)

    R.near[dp.me] = R.sums[...]
    near, near_wait = far_copies(
        dp, lambda dest, source: (R.near.at[dp.me], R.near.at[source]), R.near_send, R.near_recv
    )
    for step in range(1, size):
        near(step).start()
    near_wait()
    R.wide[mp.me] = jnp.sum(R.near[...], 0)
    far_off, far_off_wait = far_copies(
        mp, lambda dest, source: (R.wide.at[mp.me], R.wide.at[source]), R.wide_send, R.wide_recv
    )
    for step in range(1, ways):
        far_off(step).start()
    far_off_wait()
    R.totals[...] = jnp.sum(R.wide[...], 0)

    for thing in (wo, first_w, small, rows_in, weights_in):
        thing.drain()
    for step in range(1, size):
        near(step).wait_send()
    for step in range(1, ways):
        far_off(step).wait_send()


def run_layer(cap, ids, levels, noise, cot, weights, moments):
    table, w_in, ln_params, w_qkv, w_out, w_up, w_down = weights
    dp, mp = lax.axis_size("dp"), lax.axis_size("mp")
    seqs, seq_len = ids.shape
    tokens, width = noise.shape
    model = cot.shape[1]
    rin = w_in.shape[0]
    heads_w = w_qkv.shape[2]
    strip, hidden = w_up.shape
    group = tokens * mp
    spots = dp * cap
    wide = round_up(rin, 16) + 16
    far, far_dp = mp // 2, dp // 2
    quarter = model // mp
    in_kind = LOW if rin % 16 == 0 else F32
    tile_rows = max(rows for rows in range(8, 257, 8) if table.shape[0] % rows == 0)
    stacked = (heads_w // HD) * seq_len
    vmem = pl.BlockSpec(memory_space=pltpu.VMEM)
    outside = pl.BlockSpec(memory_space=pl.ANY)
    inputs = dict(
        ids=(ids, vmem),
        levels=(levels, pl.BlockSpec(memory_space=pltpu.SMEM)),
        noise=(noise, vmem),
        cot=(cot, vmem),
        table=(table, outside),
        w_in=(w_in, vmem),
        ln_params=(ln_params, vmem),
        w_qkv=(w_qkv, vmem),
        w_out=(w_out, vmem),
        w_up=(w_up, vmem),
        w_down=(w_down, vmem),
    )
    kept = {}
    for name, (first, second) in zip(("table", "w_in", "ln", "qkv", "out", "up", "down"), moments):
        inputs[name + "_m"] = (first, outside)
        inputs[name + "_v"] = (second, outside)
        if name != "table":
            kept[name + "_m_here"] = kept[name + "_v_here"] = (first.shape, F32)
    outputs = dict(
        out=((tokens, model), F32),
        red_up=((strip, hidden), F32),
        red_dn=((hidden, strip), F32),
        red_qkv=((3, strip, heads_w), F32),
        red_out=((heads_w, strip), F32),
        red_in=((rin, model), F32),
        red_ln=((4, strip), F32),
        inc=((mp * spots, width), LOW),
        named=((8, mp * spots), jnp.int32),
        totals=((8, 128), F32),
    )
    buffers = dict(
        tab=((2, round_up(table.shape[0] // 8, 128), width), F32),
        ask=((dp, 8, 128), F32),
        idx=((mp, dp, 8, 128), F32),
        loc=((spots, 128), jnp.int32),
        give=((spots, width), LOW),
        got=((spots, width), LOW),
        tw=((2, tile_rows, width), F32),
        tm=((2, tile_rows, width), F32),
        tv=((2, tile_rows, width), F32),
        sums=((8, 128), F32),
        near=((dp, 8, 128), F32),
        wide=((mp, 8, 128), F32),
        scores=((2, stacked, seq_len), F32),
        dprobs=((2, stacked, seq_len), F32),
        probs=((2, stacked, seq_len), LOW),
        dscores=((2, stacked, seq_len), LOW),
        upper=((2, stacked, heads_w), LOW),
        gwo=((model, heads_w), LOW),
        wo_first=((strip, heads_w), LOW),
        wo_second=((dp * strip, heads_w), LOW),
        gains=((8, model), F32),
        lnsum=((8, model), F32),
        sig=((tokens, 1), F32),
        pick=((tokens, spots), LOW),
        rows=((tokens, width), LOW),
        mixed=((tokens, width), LOW),
        x0=((tokens, model), F32),
        a=((group, model), LOW),
        c=((group, model), LOW),
        dx=((seqs, group // seqs, model), LOW),
        dmid=((tokens, model), F32),
        dmid_all=((group, model), LOW),
        winf=((mp, rin * dp, quarter), in_kind),
        waf=((model, 4 * heads_w), LOW),
        wbf=((model, hidden), LOW),
        wcf=((model, hidden), LOW),
        qkv=((group, 3 * heads_w), LOW),
        o=((group, heads_w), LOW),
        low=((group // seqs, heads_w), LOW),
        part=((group, model), LOW),
        first=((far * tokens, model), LOW),
        fold=((far * tokens, model), LOW),
        second=((far * tokens, model), LOW),
        fold_far=((far * tokens, model), LOW),
        h=((group // seqs, min(256, hidden)), F32),
        hb=((group, hidden), LOW),
        dhb=((group, hidden), LOW),
        slope=((group, hidden), LOW),
        gdn=((model, hidden), LOW),
        dx0=((tokens, model), LOW),
        norms=((8, model), F32),
        gm=((mp, width + 16, quarter), LOW),
        gm_first=((far, width + 16, quarter), LOW),
        gm_second=((far, width + 16, quarter), LOW),
        gw=((dp, wide, quarter), LOW),
        gw_first=((far_dp, wide, quarter), LOW),
        gw_second=((far_dp, wide, quarter), LOW),
        up_first=((far_dp * strip, hidden), LOW),
        up_second=((far_dp * strip, hidden), LOW),
        dn_first=((far_dp * strip, hidden), LOW),
        dn_second=((far_dp * strip, hidden), LOW),
        wa_first=((far_dp * strip, 3 * heads_w), LOW),
        wa_second=((far_dp * strip, 3 * heads_w), LOW),
        wsum=((mp, wide, quarter), LOW),
        up_extra=((strip, hidden), LOW),
        dn_extra=((strip, hidden), LOW),
        wa_extra=((strip, 3 * heads_w), LOW),
        gw_extra=((wide, quarter), LOW),
        **kept,
    )
    sems = dict(tab_sem=2, tile_sem=6, moment_sem=12)
    for name in (
        *("win", "wa", "wx", "wb", "wc", "wd", "ask", "give", "back"),
        *("up", "dn", "ga", "wo", "gw", "near"),
    ):
        sems[name + "_send"] = sems[name + "_recv"] = dp + 1
    for name in ("wim", "id", "in", "ws", "gm", "wide"):
        sems[name + "_send"] = sems[name + "_recv"] = mp
    for name in ("dx", "a", "c", "e"):
        sems[name + "_send"] = sems[name + "_recv"] = 2 * seqs * mp
    for name in ("as", "os", "cs", "ds"):
        sems[name + "_send"] = sems[name + "_recv"] = seqs * mp * (model // min(256, model))
    names = [*inputs, *outputs, *buffers, *sems]
    made = pl.pallas_call(
        functools.partial(layer_kernel, cap, names),
        out_shape=[jax.ShapeDtypeStruct(shape, kind) for shape, kind in outputs.values()],
        in_specs=[spec for _, spec in inputs.values()],
        out_specs=[vmem] * len(outputs),
        scratch_shapes=[
            *[pltpu.VMEM(shape, kind) for shape, kind in buffers.values()],
            *[pltpu.SemaphoreType.DMA((number,)) for number in sems.values()],
        ],
        compiler_params=pltpu.CompilerParams(
            vmem_limit_bytes=VMEM_BYTES, collective_id=1, has_side_effects=True
        ),
        name="layer",
    )(*[value for value, _ in inputs.values()])
    return dict(zip(outputs, made))


def direction_of(weight, gradient, first, second):
    first_new = BETA_ONE * first + (1.0 - BETA_ONE) * gradient
    second_new = BETA_TWO * second + (1.0 - BETA_TWO) * gradient * gradient
    second_hat = second_new * (1.0 / (1.0 - BETA_TWO**STEP))
    inverse = lax.rsqrt(second_hat)
    root = second_hat * inverse + EPS_ADAM
    inverse = inverse * (2.0 - root * inverse)
    inverse = inverse * (2.0 - root * inverse)
    direction = first_new * (1.0 / (1.0 - BETA_ONE**STEP)) * inverse + DECAY * weight
    return first_new, second_new, direction


def update_kernel(part, names, *refs):
    R = types.SimpleNamespace(**dict(zip(names, refs)))
    turn = pl.program_id(0)
    R.out_rows[...] = R.made[...]
    norms = jnp.sqrt(R.totals[...])
    R.norms[...] = norms[0:2, 0:12]
    factors = norms[0:1, :] / (norms[1:2, :] + EPS_ADAM) * RATE

    def piece(name, here, gradient, place, rows=slice(None)):
        weight = getattr(R, name)[here]
        first_new, second_new, direction = direction_of(
            weight, gradient, getattr(R, name + "_m")[here], getattr(R, name + "_v")[here]
        )
        if isinstance(place, int):
            factor = factors[0:1, place : place + 1]
        else:
            factor = jnp.concatenate([factors[0:1, one : one + 1] for one in place], 0)
        getattr(R, name + "_m_new")[here] = first_new
        getattr(R, name + "_v_new")[here] = second_new
        getattr(R, name + "_new")[here] = weight - factor * direction

    def update(name, gradient, place, lead=(), here=slice(None)):
        piece(name, (*lead, here, slice(None)), gradient, place)

    tile = R.table.shape[0]
    spots = R.named.shape[1]

    def table_part(row):
        hit = (
            lax.broadcasted_iota(jnp.int32, (part, spots), 0) + (turn * tile + row)
            == R.named[0:1, :]
        )
        gradient = dot(jnp.where(hit, 1.0, 0.0).astype(LOW), R.inc[...])
        update("table", gradient, 0, (), pl.ds(row, part))

    strips(tile, part, table_part)
    for group in range(3):
        update("qkv", R.red_qkv[group], 6 + group, (group,))
    update("up", R.red_up[...], 10)
    update("down", R.red_dn[...], 11)

    @pl.when(turn == 0)
    def _():
        update("out", R.red_out[...], 9)
        update("w_in", R.red_in[...], 1)
        piece("ln", (slice(None), slice(None)), R.red_ln[...], (2, 3, 4, 5))


def turns_of(rows, parts):
    return [
        turns
        for turns in (5, 4, 2, 1)
        if rows % (8 * turns) == 0 and all(size % (8 * turns) == 0 for size in parts)
    ][0]


def run_update(weights, moments, grads):
    names = ("table", "w_in", "ln", "qkv", "out", "up", "down")
    by_name = dict(zip(names, weights))
    rows, width = by_name["table"].shape
    strip, hidden = by_name["up"].shape
    heads_w = by_name["qkv"].shape[2]
    turns = turns_of(rows, (strip, hidden))
    tile = rows // turns
    part = max(size for size in range(8, 257, 8) if tile % size == 0)
    fixed = lambda array: pl.BlockSpec(array.shape, lambda turn: (0,) * array.ndim)
    specs = dict(
        table=pl.BlockSpec((tile, width), lambda turn: (turn, 0)),
        w_in=fixed(by_name["w_in"]),
        ln=fixed(by_name["ln"]),
        qkv=pl.BlockSpec((3, strip // turns, heads_w), lambda turn: (0, turn, 0)),
        out=fixed(by_name["out"]),
        up=pl.BlockSpec((strip // turns, hidden), lambda turn: (turn, 0)),
        down=pl.BlockSpec((hidden // turns, strip), lambda turn: (turn, 0)),
    )
    inputs = {}
    for name, weight, (first, second) in zip(names, weights, moments):
        inputs[name] = (weight, specs[name])
        inputs[name + "_m"] = (first, specs[name])
        inputs[name + "_v"] = (second, specs[name])
    for name, like in (
        ("red_up", "up"),
        ("red_dn", "down"),
        ("red_qkv", "qkv"),
        ("red_out", "out"),
        ("red_in", "w_in"),
        ("red_ln", "ln"),
    ):
        inputs[name] = (grads[name], specs[like])
    for name in ("inc", "named", "totals"):
        inputs[name] = (grads[name], fixed(grads[name]))
    tokens, model = grads["out"].shape
    rows_spec = pl.BlockSpec((tokens // turns, model), lambda turn: (turn, 0))
    inputs["made"] = (grads["out"], rows_spec)
    outputs = {"out_rows": (grads["out"].shape, rows_spec)}
    for name, weight in by_name.items():
        for kind in ("_new", "_m_new", "_v_new"):
            outputs[name + kind] = (weight.shape, specs[name])
    outputs["norms"] = ((2, 12), pl.BlockSpec((2, 12), lambda turn: (0, 0)))
    results = pl.pallas_call(
        functools.partial(update_kernel, part, [*inputs, *outputs]),
        grid=(turns,),
        out_shape=[jax.ShapeDtypeStruct(shape, F32) for shape, _ in outputs.values()],
        in_specs=[spec for _, spec in inputs.values()],
        out_specs=[spec for _, spec in outputs.values()],
        compiler_params=pltpu.CompilerParams(vmem_limit_bytes=VMEM_BYTES),
        name="update",
    )(*[value for value, _ in inputs.values()])
    return list(results)


def per_device(
    token_ids,
    levels,
    noise,
    cotangent,
    table,
    table_m,
    table_v,
    w_in,
    w_in_m,
    w_in_v,
    ln_params,
    ln_m,
    ln_v,
    w_qkv,
    qkv_m,
    qkv_v,
    w_out,
    out_m,
    out_v,
    w_up,
    up_m,
    up_v,
    w_down,
    down_m,
    down_v,
):
    dp_count = lax.axis_size("dp")
    seq_count, seq_len = token_ids.shape
    tokens = seq_count * seq_len
    model = cotangent.shape[2]
    cap = round_up(max(2, (3 * tokens + 2 * dp_count - 1) // (2 * dp_count)), 16)
    weights = (table, w_in, ln_params, w_qkv, w_out, w_up, w_down)
    moments = (
        (table_m, table_v),
        (w_in_m, w_in_v),
        (ln_m, ln_v),
        (qkv_m, qkv_v),
        (out_m, out_v),
        (up_m, up_v),
        (down_m, down_v),
    )
    grads = run_layer(
        cap,
        token_ids,
        levels,
        noise.reshape(tokens, -1),
        cotangent.reshape(tokens, model),
        weights,
        moments,
    )
    out, *results = run_update(weights, moments, grads)
    return (out.reshape(seq_count, seq_len, model), *results)


def solution(mesh):
    return jax.shard_map(
        per_device,
        mesh=mesh,
        in_specs=(
            P(("dp", "mp"), None),
            P(("dp", "mp")),
            P(("dp", "mp"), None, None),
            P(("dp", "mp"), None, None),
            P("dp", None),
            P("dp", None),
            P("dp", None),
            P("dp", None),
            P("dp", None),
            P("dp", None),
            P(None, "dp"),
            P(None, "dp"),
            P(None, "dp"),
            P(None, "dp", "mp"),
            P(None, "dp", "mp"),
            P(None, "dp", "mp"),
            P("mp", "dp"),
            P("mp", "dp"),
            P("mp", "dp"),
            P("dp", "mp"),
            P("dp", "mp"),
            P("dp", "mp"),
            P("mp", "dp"),
            P("mp", "dp"),
            P("mp", "dp"),
        ),
        out_specs=(
            P(("dp", "mp"), None, None),
            P("dp", None),
            P("dp", None),
            P("dp", None),
            P("dp", None),
            P("dp", None),
            P("dp", None),
            P(None, "dp"),
            P(None, "dp"),
            P(None, "dp"),
            P(None, "dp", "mp"),
            P(None, "dp", "mp"),
            P(None, "dp", "mp"),
            P("mp", "dp"),
            P("mp", "dp"),
            P("mp", "dp"),
            P("dp", "mp"),
            P("dp", "mp"),
            P("dp", "mp"),
            P("mp", "dp"),
            P("mp", "dp"),
            P("mp", "dp"),
            P(),
        ),
        check_vma=False,
    )
```

profile of v0, /device:TPU:0, one launch (start us, length us, event | category | flops | bytes accessed | tf_op | source)
XLA Modules:
  0.0 207.7 jit_solution(5835179065960345980)
XLA Ops:
  0.7 188.3 %layer.1 = (f32[256,1024]{1,0:T(8,128)}, f32[128,1024]{1,0:T(8,128)}, f32[1024,128]{1,0:T(8,128)}, f32[3,128,256]{2,1,0:T(8,128)}, f32[256,128]{1,0:T(8,128)}, /...) custom-call(s32[2,128]{1,0:T(2,128)} %refs_0_.2, ...), custom_call_target="tpu_custom_call" | custom-call | tf_op jit(solution)/shard_map/layer/pallas_call | solution.py:1674
  189.0 18.5 %update.1 = (f32[256,1024]{1,0:T(8,128)}, f32[4000,256]{1,0:T(8,128)}, f32[4000,256]{1,0:T(8,128)}, f32[4000,256]{1,0:T(8,128)}, f32[32,1024]{1,0:T(8,128)}, /*i...) custom-call(f32[4000,256]{1,0:T(8,128)} %refs_0_.3, ...), custom_call_target="tpu_custom_call" | custom-call | tf_op jit(solution)/shard_map/update/pallas_call | solution.py:1802
where the time goes:
time: 208 us
  Pallas kernels  207 us (100%)
    pallas_call x1, Pallas kernels, run_layer(): pl.pallas_call(functools.partial(layer_kernel, cap, names), out_shape=[ja...  188 us
    pallas_call x1, Pallas kernels, run_update(): pl.pallas_call(functools.partial(update_kernel, part, [*inputs, *outputs]...  18.5 us

commit v1 on v0

--- a/solution.py
+++ b/solution.py
@@ -729,6 +729,12 @@
         name + kind for name in ("w_in", "ln", "qkv", "out", "up", "down") for kind in ("_m", "_v")
     ]
 
+    def store(name):
+        place = ("out", "red_up", "red_dn", "red_qkv", "inc").index(name)
+        return pltpu.make_async_copy(
+            getattr(R, name), getattr(R, name + "_hbm"), R.store_sem.at[place]
+        )
+
     def moment(name):
         return pltpu.make_async_copy(
             getattr(R, name), getattr(R, name + "_here"), R.moment_sem.at[names_of_moments.index(name)]
@@ -807,15 +813,7 @@
         R.wo_send,
         R.wo_recv,
     )
-    small = Scatter(
-        dp,
-        *[of_index(ref) for ref in (R.gw, R.gw_first, R.gw_second)],
-        R.gw_send,
-        R.gw_recv,
-        0,
-        R.gw_extra,
-    )
-    for scatter in (up, down, first_w, small):
+    for scatter in (up, down, first_w):
         scatter.clear()
 
     meet([mp], [dp])
@@ -859,10 +857,6 @@
     R.waf[own_strip, 3 * heads_w :] = R.w_out[...].T.astype(LOW)
     wa[0].start()
     wa[1].start_near()
-    for name in names_of_moments:
-        moment(name).start()
-
-    win.relays()
 
     ask_wait()
     small_eye = lax.broadcasted_iota(jnp.int32, (cap, 128), 0) == lax.broadcasted_iota(
@@ -877,6 +871,7 @@
         return carry
 
     lax.fori_loop(0, size, locate, 0, unroll=True)
+    win.relays()
     found = None
     for piece in range(pieces):
         fetch(piece).wait()
@@ -902,6 +897,10 @@
         give(step).start()
     R.got[mine, :] = R.give[mine, :]
     wa[1].start_far()
+    named = Gather(mp, of_index(R.idx), R.id_send, R.id_recv)
+    named.start()
+    for name in names_of_moments:
+        moment(name).start()
     win.close()
     win_all.start()
     wa[0].relay(1)
@@ -929,6 +928,7 @@
         lax.broadcasted_iota(jnp.int32, (tokens, spots), 1).astype(F32) == slot, 1.0, 0.0
     ).astype(LOW)
     win_all.relays()
+    named.relays()
     wa[0].relay(2)
     if wide_ln % 128 == 0:
         R.gains[...] = jnp.concatenate([R.idx[mp.me, index] for index in range(size)], 1)
@@ -945,7 +945,6 @@
         R.gains[...] = total
     for step in range(3, dp.far):
         wa[0].relay(step)
-    named = Gather(mp, of_index(R.idx), R.id_send, R.id_recv)
 
     give_wait()
     rows = dot(R.pick[...], R.got[...])
@@ -973,174 +972,6 @@
         wa[1].relay(step)
     dxg.relays()
     ag[0].relays()
-    for gather in (*wa, ag[0]):
-        gather.close()
-
-    att = Sums(R.part, R.fold, R.fold_far, R.as_send, R.as_recv)
-    dcs = Sums(R.part, R.fold, R.fold_far, R.cs_send, R.cs_recv)
-    das = Sums(R.part, R.fold, R.fold_far, R.ds_send, R.ds_recv)
-    out = Sums(R.c, R.first, R.second, R.os_send, R.os_recv)
-    masks = head_masks(heads_w)
-
-    all_rows = (heads_w // HD) * seq_len
-    scale = HD ** (-0.5)
-
-    def softmax(seq, row):
-        scores = R.scores[seq, row : row + 64, :]
-        raised = jnp.exp((scores - jnp.max(scores, -1, keepdims=True)) * scale)
-        return raised * (1.0 / jnp.sum(raised, -1, keepdims=True))
-
-    def attend(piece, base, here, at):
-        at("start")
-        for part in range(3):
-            cols = slice(part * heads_w, (part + 1) * heads_w)
-            R.qkv[here, cols] = dot(R.a[here, :], R.waf[:, cols]).astype(LOW)
-        at("mid")
-
-        def one(rows_at):
-            for seq, rows in enumerate(rows_at):
-                queries = spread_heads(R.qkv[rows, :heads_w], masks)
-                R.scores[seq] = dot_nt(queries, R.qkv[rows, heads_w : 2 * heads_w])
-            for seq, rows in enumerate(rows_at):
-                for row in range(0, all_rows, 64):
-                    R.probs[seq, row : row + 64, :] = softmax(seq, row).astype(LOW)
-                seen = dot(R.probs[seq], R.qkv[rows, 2 * heads_w : 3 * heads_w])
-                R.o[rows, :] = join_heads(seen, masks, seq_len).astype(LOW)
-
-        pairs(base, one)
-        at("late")
-
-        def project(cols):
-            R.part[here, cols] = dot_nt(R.o[here, :], R.waf[cols, 3 * heads_w :]).astype(LOW)
-
-        def one_chunk(chunk, carry):
-            project(pl.ds(pl.multiple_of(chunk * chunk_cols, chunk_cols), chunk_cols))
-            att.trade(piece, chunk)
-            return carry
-
-        lax.fori_loop(0, chunk_count, one_chunk, 0)
-
-    def second_norm(piece):
-        here, there = rows_of(piece), own_rows(piece)
-        att.arrive(piece)
-
-        def norm(row):
-            x1 = R.x0[here(row), :] + att.total(piece, pl.ds(row, some_rows))
-            R.out[here(row), :] = x1
-            normed, _ = norm_rows(x1)
-            R.c[there(row), :] = (normed * R.gains[3:4, :] + R.gains[4:5, :]).astype(LOW)
-
-        by_rows(norm, cg[piece].start)
-
-    def first_wb():
-        wb.relay(1)
-        wd.start_near()
-        wc.start_near()
-        wc.start_far()
-
-    def middle_wb():
-        wb.relay(2)
-        wd.start_far()
-
-    def last_wb():
-        wd.start_other()
-        for step in range(3, dp.far):
-            wb.relay(step)
-        named.start()
-
-    turns(
-        attend,
-        [
-            *later_pieces(ag, "mid"),
-            *[
-                (piece + 1, "mid", functools.partial(att.hand_on_all, piece))
-                for piece in range(seqs - 1)
-            ],
-            (0, "mid", first_wb),
-            (0, "late", middle_wb),
-            (1, "mid", last_wb),
-            *[
-                (piece + 1, "late", functools.partial(second_norm, piece))
-                for piece in range(seqs - 1)
-            ],
-        ],
-    )
-    att.hand_on_all(seqs - 1)
-    wc.relay(1)
-    for gather in (*wa, *ag, dxg, win):
-        gather.drain()
-    for step in range(1, size):
-        ask(step).wait_send()
-    second_norm(seqs - 1)
-    cg[0].relays()
-    wc.relay(2)
-    wb.close()
-    named.relays()
-    cg[0].close()
-    for piece in range(seqs):
-        att.drain(piece)
-
-    def activate(piece, base, here, at):
-        at("start")
-
-        def some(cols):
-            R.h[...] = dot(R.c[here, :], R.wbf[:, cols])
-
-            def gelu(row):
-                there = pl.ds(pl.multiple_of(base + row, 64), 64)
-                h = R.h[pl.ds(row, 64), :]
-                bell = jnp.exp(-0.5 * h * h)
-                tail = normal_tail(jnp.abs(h), bell)
-                gate = jnp.where(h >= 0.0, 1.0 - tail, tail)
-                slope = gate + h * (bell * 0.3989422804014327)
-                R.hb[there, cols] = (h * gate).astype(LOW)
-                R.slope[there, cols] = slope.astype(LOW)
-
-            strips(many, 64, gelu, 2)
-
-        chunks(hidden, some)
-        at("end")
-
-    def last_wc():
-        for step in range(3, dp.far):
-            wc.relay(step)
-
-    turns(activate, [*later_pieces(cg, "end"), (0, "end", last_wc), (seqs - 1, "start", wd.forward)])
-
-    due = [(scatter, step) for scatter in (down, up) for step in range(1, dp.far)]
-
-    def pass_due(number):
-        for _ in range(min(number, len(due))):
-            scatter, step = due.pop(0)
-            scatter.pass_on(step)
-
-    block = 2 * strip if (2 * strip) % 128 == 0 else min(256, model)
-
-    def grads(make, trades):
-        if block == 2 * strip:
-
-            def turn_of(turn, carry):
-                hi = up.turn_of(turn)
-                make(pl.ds(pl.multiple_of(hi * block, block), block))
-                for scatter in trades:
-                    scatter.trade(hi)
-                return carry
-
-            lax.fori_loop(0, dp.far, turn_of, 0)
-        else:
-            strips(model, block, lambda col: make(pl.ds(col, block)))
-            for scatter in trades:
-                scatter.trade_all()
-
-    def down_grads(cols):
-        every = R.dx[:, :, cols]
-        R.gdn[cols, :] = dot_tn(every.reshape(seqs * many, block), R.hb[...]).astype(LOW)
-
-    def up_grads(cols):
-        R.wbf[cols, :] = dot_tn(R.c[:, cols], R.dhb[...]).astype(LOW)
-
-    dxg.close()
-    grads(down_grads, (down,))
     named.close()
     groups = ways * size
     some, lanes_at = min(groups, 32), min(ways * spots, 512)
@@ -1169,6 +1000,172 @@
             named_row.astype(jnp.int32) - dp.me * table_rows, (8, lanes_at)
         )
     named.drain()
+    for gather in (*wa, ag[0]):
+        gather.close()
+
+    att = Sums(R.part, R.fold, R.fold_far, R.as_send, R.as_recv)
+    dcs = Sums(R.part, R.fold, R.fold_far, R.cs_send, R.cs_recv)
+    das = Sums(R.part, R.fold, R.fold_far, R.ds_send, R.ds_recv)
+    out = Sums(R.c, R.first, R.second, R.os_send, R.os_recv)
+    masks = head_masks(heads_w)
+
+    all_rows = (heads_w // HD) * seq_len
+    scale = HD ** (-0.5)
+
+    def softmax(seq, row):
+        scores = R.scores[seq, row : row + 64, :]
+        raised = jnp.exp((scores - jnp.max(scores, -1, keepdims=True)) * scale)
+        return raised * (1.0 / jnp.sum(raised, -1, keepdims=True))
+
+    def attend(piece, base, here, at):
+        at("start")
+        for part in range(3):
+            cols = slice(part * heads_w, (part + 1) * heads_w)
+            R.qkv[here, cols] = dot(R.a[here, :], R.waf[:, cols]).astype(LOW)
+        at("mid")
+
+        def one(rows_at):
+            for seq, rows in enumerate(rows_at):
+                queries = spread_heads(R.qkv[rows, :heads_w], masks)
+                R.scores[seq] = dot_nt(queries, R.qkv[rows, heads_w : 2 * heads_w])
+            for seq, rows in enumerate(rows_at):
+                for row in range(0, all_rows, 64):
+                    R.probs[seq, row : row + 64, :] = softmax(seq, row).astype(LOW)
+                seen = dot(R.probs[seq], R.qkv[rows, 2 * heads_w : 3 * heads_w])
+                R.o[rows, :] = join_heads(seen, masks, seq_len).astype(LOW)
+
+        pairs(base, one)
+        at("late")
+
+        def project(cols):
+            R.part[here, cols] = dot_nt(R.o[here, :], R.waf[cols, 3 * heads_w :]).astype(LOW)
+
+        def one_chunk(chunk, carry):
+            project(pl.ds(pl.multiple_of(chunk * chunk_cols, chunk_cols), chunk_cols))
+            att.trade(piece, chunk)
+            return carry
+
+        lax.fori_loop(0, chunk_count, one_chunk, 0)
+
+    def second_norm(piece):
+        here, there = rows_of(piece), own_rows(piece)
+        att.arrive(piece)
+
+        def norm(row):
+            x1 = R.x0[here(row), :] + att.total(piece, pl.ds(row, some_rows))
+            R.out[here(row), :] = x1
+            normed, _ = norm_rows(x1)
+            R.c[there(row), :] = (normed * R.gains[3:4, :] + R.gains[4:5, :]).astype(LOW)
+
+        by_rows(norm, cg[piece].start)
+
+    def first_wb():
+        wb.relay(1)
+        wd.start_near()
+        wc.start_near()
+        wc.start_far()
+
+    def middle_wb():
+        wb.relay(2)
+        wd.start_far()
+
+    def last_wb():
+        wd.start_other()
+        for step in range(3, dp.far):
+            wb.relay(step)
+
+    turns(
+        attend,
+        [
+            *later_pieces(ag, "mid"),
+            *[
+                (piece + 1, "mid", functools.partial(att.hand_on_all, piece))
+                for piece in range(seqs - 1)
+            ],
+            (0, "mid", first_wb),
+            (0, "late", middle_wb),
+            (1, "mid", last_wb),
+            *[
+                (piece + 1, "late", functools.partial(second_norm, piece))
+                for piece in range(seqs - 1)
+            ],
+        ],
+    )
+    att.hand_on_all(seqs - 1)
+    wc.relay(1)
+    for gather in (*wa, *ag, dxg, win):
+        gather.drain()
+    for step in range(1, size):
+        ask(step).wait_send()
+    second_norm(seqs - 1)
+    cg[0].relays()
+    wc.relay(2)
+    wb.close()
+    cg[0].close()
+    for piece in range(seqs):
+        att.drain(piece)
+
+    def activate(piece, base, here, at):
+        at("start")
+
+        def some(cols):
+            R.h[...] = dot(R.c[here, :], R.wbf[:, cols])
+
+            def gelu(row):
+                there = pl.ds(pl.multiple_of(base + row, 64), 64)
+                h = R.h[pl.ds(row, 64), :]
+                bell = jnp.exp(-0.5 * h * h)
+                tail = normal_tail(jnp.abs(h), bell)
+                gate = jnp.where(h >= 0.0, 1.0 - tail, tail)
+                slope = gate + h * (bell * 0.3989422804014327)
+                R.hb[there, cols] = (h * gate).astype(LOW)
+                R.slope[there, cols] = slope.astype(LOW)
+
+            strips(many, 64, gelu, 2)
+
+        chunks(hidden, some)
+        at("end")
+
+    def last_wc():
+        for step in range(3, dp.far):
+            wc.relay(step)
+
+    turns(activate, [*later_pieces(cg, "end"), (0, "end", last_wc), (seqs - 1, "start", wd.forward)])
+
+    due = [(scatter, step) for scatter in (down, up) for step in range(1, dp.far)]
+
+    def pass_due(number):
+        for _ in range(min(number, len(due))):
+            scatter, step = due.pop(0)
+            scatter.pass_on(step)
+
+    block = 2 * strip if (2 * strip) % 128 == 0 else min(256, model)
+
+    def grads(make, trades):
+        if block == 2 * strip:
+
+            def turn_of(turn, carry):
+                hi = up.turn_of(turn)
+                make(pl.ds(pl.multiple_of(hi * block, block), block))
+                for scatter in trades:
+                    scatter.trade(hi)
+                return carry
+
+            lax.fori_loop(0, dp.far, turn_of, 0)
+        else:
+            strips(model, block, lambda col: make(pl.ds(col, block)))
+            for scatter in trades:
+                scatter.trade_all()
+
+    def down_grads(cols):
+        every = R.dx[:, :, cols]
+        R.gdn[cols, :] = dot_tn(every.reshape(seqs * many, block), R.hb[...]).astype(LOW)
+
+    def up_grads(cols):
+        R.wbf[cols, :] = dot_tn(R.c[:, cols], R.dhb[...]).astype(LOW)
+
+    dxg.close()
+    grads(down_grads, (down,))
     wc.close()
     wd.close()
     for gather in (wb, *cg):
@@ -1303,10 +1300,11 @@
     def attend_grads(cols):
         R.waf[cols, : 3 * heads_w] = dot_tn(R.a[:, cols], R.qkv[...]).astype(LOW)
 
+    first_back(0)
+    pass_due(len(due))
+    grads(attend_grads, (first_w,))
     grads(out_grads, ())
     wo.start()
-    first_back(0)
-    grads(attend_grads, (first_w,))
     for piece in range(1, seqs):
         first_back(piece)
 
@@ -1344,7 +1342,6 @@
             [R.norms[0:4, cols], jnp.zeros((12, quarter), F32)], 0
         ).astype(LOW)
     small_mp.trade_all()
-    pass_due(len(due))
     for step in range(1, far):
         small_mp.pass_on(step)
 
@@ -1376,7 +1373,12 @@
             piece = jnp.concatenate([piece, jnp.zeros((rin_up - rin, quarter), F32)], 0)
         R.gw[index, :rin_up, :] = piece.astype(LOW)
         R.gw[index, rin_up:, :] = summed[width:, :].astype(LOW)
-    small.trade_all()
+    R.gw_in[dp.me] = R.gw[dp.me]
+    small, small_wait = far_copies(
+        dp, lambda dest, source: (R.gw.at[dest], R.gw_in.at[source]), R.gw_send, R.gw_recv
+    )
+    for step in range(1, size):
+        small(step).start()
     rows_in.relays()
     for step in range(3, dp.far):
         first_w.pass_on(step)
@@ -1394,8 +1396,10 @@
 
     for piece in range(seqs):
         finish_out(piece)
+    store("out").start()
 
     rows_in.close()
+    store("inc").start()
 
     once = jnp.where(mp.me == 0, 1.0, 0.0)
     lanes = lax.broadcasted_iota(jnp.int32, (1, 128), 1)
@@ -1422,20 +1426,8 @@
 
     zero = jnp.zeros((8, width), F32)
 
-    rest = [
-        functools.partial(scatter.pass_on, step)
-        for scatter in (small,)
-        for step in range(1, dp.far)
-    ]
-    tail_hooks = [
-        (min(shares_of - 1, place * shares_of // len(rest)), action)
-        for place, action in enumerate(rest)
-    ]
-
     def add_tile(turn, carry):
         side = lax.rem(turn, 2)
-        for place, action in tail_hooks:
-            pl.when(turn == place)(action)
         for one in tile_of(turn):
             one.wait()
         hit = (
@@ -1469,17 +1461,19 @@
     up.arrive()
 
     R.red_up[...] = up.total(slice(None))
+    store("red_up").start()
     put(10, add_up(R.w_up, R.red_up, R.up_m_here, R.up_v_here))
     down.arrive()
 
     R.red_dn[...] = down.total(slice(None)).T
+    store("red_dn").start()
     put(11, add_up(R.w_down, R.red_dn, R.down_m_here, R.down_v_here))
     wo.arrive()
     R.red_out[...] = wo.total().T
     put(9, add_up(R.w_out, R.red_out, R.out_m_here, R.out_v_here))
 
-    small.arrive()
-    R.wsum[mp.me] = small.total(slice(None)).astype(LOW)
+    small_wait()
+    R.wsum[mp.me] = jnp.sum(R.gw_in[...].astype(F32), 0).astype(LOW)
     weights_in = Gather(mp, of_index(R.wsum), R.ws_send, R.ws_recv)
     weights_in.start()
     first_w.arrive()
@@ -1487,6 +1481,7 @@
     value = first_w.total(slice(None))
     for part in range(3):
         R.red_qkv[part] = value[:, part * heads_w : (part + 1) * heads_w]
+    store("red_qkv").start()
     weights_in.relays()
     for part in range(3):
         put(
@@ -1529,12 +1524,15 @@
     far_off_wait()
     R.totals[...] = jnp.sum(R.wide[...], 0)
 
-    for thing in (wo, first_w, small, rows_in, weights_in):
+    for thing in (wo, first_w, rows_in, weights_in):
         thing.drain()
     for step in range(1, size):
         near(step).wait_send()
+        small(step).wait_send()
     for step in range(1, ways):
         far_off(step).wait_send()
+    for name in ("out", "red_up", "red_dn", "red_qkv", "inc"):
+        store(name).wait()
 
 
 def run_layer(cap, ids, levels, noise, cot, weights, moments):
@@ -1575,15 +1573,18 @@
         inputs[name + "_v"] = (second, outside)
         if name != "table":
             kept[name + "_m_here"] = kept[name + "_v_here"] = (first.shape, F32)
-    outputs = dict(
+    own_stores = dict(
         out=((tokens, model), F32),
         red_up=((strip, hidden), F32),
         red_dn=((hidden, strip), F32),
         red_qkv=((3, strip, heads_w), F32),
+        inc=((mp * spots, width), LOW),
+    )
+    outputs = dict(
+        **{name + "_hbm": shape for name, shape in own_stores.items()},
         red_out=((heads_w, strip), F32),
         red_in=((rin, model), F32),
         red_ln=((4, strip), F32),
-        inc=((mp * spots, width), LOW),
         named=((8, mp * spots), jnp.int32),
         totals=((8, 128), F32),
     )
@@ -1643,8 +1644,7 @@
         gm_first=((far, width + 16, quarter), LOW),
         gm_second=((far, width + 16, quarter), LOW),
         gw=((dp, wide, quarter), LOW),
-        gw_first=((far_dp, wide, quarter), LOW),
-        gw_second=((far_dp, wide, quarter), LOW),
+        gw_in=((dp, wide, quarter), LOW),
         up_first=((far_dp * strip, hidden), LOW),
         up_second=((far_dp * strip, hidden), LOW),
         dn_first=((far_dp * strip, hidden), LOW),
@@ -1655,10 +1655,10 @@
         up_extra=((strip, hidden), LOW),
         dn_extra=((strip, hidden), LOW),
         wa_extra=((strip, 3 * heads_w), LOW),
-        gw_extra=((wide, quarter), LOW),
         **kept,
-    )
-    sems = dict(tab_sem=2, tile_sem=6, moment_sem=12)
+        **own_stores,
+    )
+    sems = dict(store_sem=5, tab_sem=2, tile_sem=6, moment_sem=12)
     for name in (
         *("win", "wa", "wx", "wb", "wc", "wd", "ask", "give", "back"),
         *("up", "dn", "ga", "wo", "gw", "near"),
@@ -1675,7 +1675,7 @@
         functools.partial(layer_kernel, cap, names),
         out_shape=[jax.ShapeDtypeStruct(shape, kind) for shape, kind in outputs.values()],
         in_specs=[spec for _, spec in inputs.values()],
-        out_specs=[vmem] * len(outputs),
+        out_specs=[outside if name.endswith("_hbm") else vmem for name in outputs],
         scratch_shapes=[
             *[pltpu.VMEM(shape, kind) for shape, kind in buffers.values()],
             *[pltpu.SemaphoreType.DMA((number,)) for number in sems.values()],
@@ -1685,7 +1685,7 @@
         ),
         name="layer",
     )(*[value for value, _ in inputs.values()])
-    return dict(zip(outputs, made))
+    return {name.removesuffix("_hbm"): value for name, value in zip(outputs, made)}
 
 
 def direction_of(weight, gradient, first, second):

time: 208 us -> 209 us (level)
  no operation moved by 1% of the time
where the time goes in v1:
time: 209 us; the launch traced here: 208 us
  Pallas kernels  208 us (100%)
    pallas_call x1, Pallas kernels, run_layer(): pl.pallas_call(functools.partial(layer_kernel, cap, names), out_shape=[ja...  189 us
    pallas_call x1, Pallas kernels, run_update(): pl.pallas_call(functools.partial(update_kernel, part, [*inputs, *outputs]...  18.5 us

profile of v1, /device:TPU:0, one launch (start us, length us, event | category | flops | bytes accessed | tf_op | source)
XLA Modules:
  0.0 208.4 jit_solution(7978665247116677598)
XLA Ops:
  0.7 189.0 %layer.1 = (f32[256,1024]{1,0:T(8,128)}, f32[128,1024]{1,0:T(8,128)}, f32[1024,128]{1,0:T(8,128)}, f32[3,128,256]{2,1,0:T(8,128)}, bf16[1536,256]{1,0:T(8,128)(2...) custom-call(s32[2,128]{1,0:T(2,128)} %refs_0_.2, ...), custom_call_target="tpu_custom_call" | custom-call | tf_op jit(solution)/shard_map/layer/pallas_call | solution.py:1674
  189.7 18.5 %update.1 = (f32[256,1024]{1,0:T(8,128)}, f32[4000,256]{1,0:T(8,128)}, f32[4000,256]{1,0:T(8,128)}, f32[4000,256]{1,0:T(8,128)}, f32[32,1024]{1,0:T(8,128)}, /*i...) custom-call(f32[4000,256]{1,0:T(8,128)} %refs_0_.3, ...), custom_call_target="tpu_custom_call" | custom-call | tf_op jit(solution)/shard_map/update/pallas_call | solution.py:1802
